TPU v7x, 1024 devices: a whole 8x8x8 slice. The times are simulated.
1024 devices in a mesh: dp: 2 (over core), expert: 64 (over z, y), tensor: 8 (over x).
Axes of the slice: x: 8, y: 8, z: 8, core: 2. Of those that a mesh axis runs over, the one named last changes fastest.
Arguments:
- tokens: bfloat16 [4096, 8192], P(('dp', 'expert')), may hold values from -6 to 6
- w_latent: bfloat16 [8192, 2048], P(None, 'tensor'), may hold values from -0.0625 to 0.0625
- w_gate: bfloat16 [64, 2048, 2048], P('expert', None, 'tensor'), may hold values from -0.125 to 0.125
- w_up: bfloat16 [64, 2048, 2048], P('expert', None, 'tensor'), may hold values from -0.125 to 0.125
- w_out: bfloat16 [64, 2048, 2048], P('expert', 'tensor'), may hold values from -0.125 to 0.125
- expert_ids: int32 [4096, 8], P(('dp', 'expert')), may hold values from 0 to 63, all different within a row; in each aligned block of 32 rows (0 to 31, 32 to 63, ...) at most 6 rows name the same one
- gates: bfloat16 [4096, 8], P(('dp', 'expert')), may hold values from 0.049804688 to 1
- cotangent: bfloat16 [4096, 2048], P(('dp', 'expert'), 'tensor'), may hold values from -6 to 6
Outputs:
- latent_out: bfloat16 [4096, 2048], P(('dp', 'expert'), 'tensor')
- latent_grad: bfloat16 [4096, 2048], P(('dp', 'expert'), 'tensor')
- grad_gate: bfloat16 [64, 2048, 2048], P('expert', 'dp', 'tensor')
- grad_up: bfloat16 [64, 2048, 2048], P('expert', 'dp', 'tensor')
- grad_out: bfloat16 [64, 2048, 2048], P('expert', 'tensor', 'dp')
Inputs may be any that keep to these rules, and one draw needn't show every extreme that they name: `expert_ids`: each row names 8 different experts. In each aligned block of 32 rows (the rows of one data group) no expert is named by more than 6 rows, and in some blocks one expert is named by exactly 6.
All inputs are finite; a program needn't handle non-finite values.
Results may differ from a plain program's by a relative error of at most 0.0095.
Values may be sent and summed in bfloat16 or wider, within the bound.
A program may use at most 64 MiB of HBM per device.

v0:
```python
import jax
import jax.numpy as jnp
from jax import lax
from jax.sharding import PartitionSpec as P


def per_device(tokens, w_latent, w_gate, w_up, w_out, expert_ids, gates, cotangent):
    tok_count, top_count = expert_ids.shape
    held_experts = w_gate.shape[0]
    groups = lax.axis_size("expert")
    experts_all = held_experts * groups
    capacity = 3 * tok_count * top_count // (2 * experts_all)
    slot_count = experts_all * capacity
    latent_cols = jnp.dot(tokens, w_latent, preferred_element_type=jnp.float32).astype(jnp.bfloat16)
    flat_ids = expert_ids.reshape(-1)
    member = (flat_ids[:, None] == jnp.arange(experts_all, dtype=jnp.int32)[None, :]).astype(
        jnp.int32
    )
    running = jnp.cumsum(member, axis=0) - 1
    position = jnp.sum(running * member, axis=1)
    target = flat_ids * capacity + position
    pair_hot = target[:, None] == jnp.arange(slot_count, dtype=jnp.int32)[None, :]
    placed = jnp.sum(
        pair_hot.reshape(tok_count, top_count, slot_count).astype(jnp.float32), axis=1
    ).astype(jnp.bfloat16)
    gate_slot = jnp.sum(
        jnp.where(pair_hot, gates.reshape(-1)[:, None].astype(jnp.float32), 0.0), axis=0
    ).astype(jnp.bfloat16)
    source_rows, source_cot = (
        lax.all_gather(latent_cols, "tensor", axis=1, tiled=True),
        lax.all_gather(cotangent, "tensor", axis=1, tiled=True),
    )
    width_sent = source_rows.shape[1]

    def to_slots(values):
        spread = jnp.einsum("js,jl->sl", placed, values, preferred_element_type=jnp.float32)
        return spread.astype(jnp.bfloat16).reshape(groups, held_experts * capacity, width_sent)

    slot_rows, slot_cot, slot_gate = (
        lax.all_to_all(to_slots(source_rows), "expert", split_axis=0, concat_axis=0, tiled=True),
        lax.all_to_all(to_slots(source_cot), "expert", split_axis=0, concat_axis=0, tiled=True),
        lax.all_to_all(
            gate_slot.reshape(groups, held_experts * capacity),
            "expert",
            split_axis=0,
            concat_axis=0,
            tiled=True,
        ),
    )
    latent_width = slot_rows.shape[2]
    slot_latent = slot_rows.reshape(groups, held_experts, capacity, latent_width)
    slot_cotangent = slot_cot.reshape(groups, held_experts, capacity, latent_width)
    slot_weight = slot_gate.reshape(groups, held_experts, capacity, 1).astype(jnp.float32)
    pre_gate = jnp.einsum("sxcl,xlh->sxch", slot_latent, w_gate, preferred_element_type=jnp.float32)
    pre_up = jnp.einsum("sxcl,xlh->sxch", slot_latent, w_up, preferred_element_type=jnp.float32)
    gate_sigmoid = jax.nn.sigmoid(pre_gate)
    gate_silu = pre_gate * gate_sigmoid
    activated = (gate_silu * pre_up).astype(jnp.bfloat16)
    partial_out = slot_weight * jnp.einsum(
        "sxch,xhl->sxcl", activated, w_out, preferred_element_type=jnp.float32
    )
    out_grad = (slot_weight * slot_cotangent.astype(jnp.float32)).astype(jnp.bfloat16)
    act_grad = jnp.einsum("sxcl,xhl->sxch", out_grad, w_out, preferred_element_type=jnp.float32)
    gate_grad = (act_grad * pre_up * gate_sigmoid * (1.0 + pre_gate * (1.0 - gate_sigmoid))).astype(
        jnp.bfloat16
    )
    up_grad = (act_grad * gate_silu).astype(jnp.bfloat16)
    partial_back = jnp.einsum(
        "sxch,xlh->sxcl", gate_grad, w_gate, preferred_element_type=jnp.float32
    ) + jnp.einsum("sxch,xlh->sxcl", up_grad, w_up, preferred_element_type=jnp.float32)
    summed_out, summed_back = (
        lax.psum_scatter(partial_out, "tensor", scatter_dimension=3, tiled=True),
        lax.psum_scatter(partial_back, "tensor", scatter_dimension=3, tiled=True),
    )

    def to_home(values):
        return values.astype(jnp.bfloat16).reshape(groups, held_experts * capacity, values.shape[3])

    home_out, home_back = (
        lax.all_to_all(to_home(summed_out), "expert", split_axis=0, concat_axis=0, tiled=True),
        lax.all_to_all(to_home(summed_back), "expert", split_axis=0, concat_axis=0, tiled=True),
    )
    latent_out = jnp.dot(
        placed, home_out.reshape(slot_count, -1), preferred_element_type=jnp.float32
    ).astype(jnp.bfloat16)
    latent_grad = jnp.dot(
        placed, home_back.reshape(slot_count, -1), preferred_element_type=jnp.float32
    ).astype(jnp.bfloat16)
    wide_gate = jnp.einsum(
        "sxcl,sxch->xlh", slot_latent, gate_grad, preferred_element_type=jnp.float32
    )
    wide_up = jnp.einsum("sxcl,sxch->xlh", slot_latent, up_grad, preferred_element_type=jnp.float32)
    wide_out = jnp.einsum("sxch,sxcl->xhl", activated, out_grad, preferred_element_type=jnp.float32)
    grad_gate, grad_up, grad_out = (
        lax.psum_scatter(wide_gate, "dp", scatter_dimension=1, tiled=True),
        lax.psum_scatter(wide_up, "dp", scatter_dimension=1, tiled=True),
        lax.psum_scatter(wide_out, "dp", scatter_dimension=2, tiled=True),
    )
    return (
        latent_out,
        latent_grad,
        grad_gate.astype(jnp.bfloat16),
        grad_up.astype(jnp.bfloat16),
        grad_out.astype(jnp.bfloat16),
    )


def solution(mesh):
    in_specs = (
        P(("dp", "expert"), None),
        P(None, "tensor"),
        P("expert", None, "tensor"),
        P("expert", None, "tensor"),
        P("expert", "tensor", None),
        P(("dp", "expert"), None),
        P(("dp", "expert"), None),
        P(("dp", "expert"), "tensor"),
    )
    out_specs = (
        P(("dp", "expert"), "tensor"),
        P(("dp", "expert"), "tensor"),
        P("expert", "dp", "tensor"),
        P("expert", "dp", "tensor"),
        P("expert", "tensor", "dp"),
    )
    return jax.shard_map(
        per_device, mesh=mesh, in_specs=in_specs, out_specs=out_specs, check_vma=False
    )
```

profile of v0, /device:TPU:1, one launch (start us, length us, event | category | flops | bytes accessed | tf_op | source)
XLA Modules:
  0.0 386.9 jit_solution(5392508138386311135)
XLA Ops:
  11.0 24.0 %all-to-all-start = ((bf16[64,1,6]{2,1,0:T(2,128)(2,1)}), bf16[64,1,6]{2,1,0:T(2,128)(2,1)S(1)}, u32[]{:S(2)}, u32[]{:S(2)}) async-start(bf16[64,1,6]{2,1,0:T(2,128)(2,1)} %convert_element_type.120), calls=%async_computation | async-start | bytes 65536 | tf_op jit(solution)/shard_map/all_to_all | solution.py:42
  35.2 3.2 convolution_convert_fusion.4
  38.4 19.9 %all_gather.6 = bf16[32,2048]{1,0:T(8,128)(2,1)S(1)} all-gather(bf16[32,256]{1,0:T(8,128)(2,1)S(1)} %convolution_convert_fusion.4), channel_id=1, replica_groups=mesh['dp'=2,'expert'=64,'tensor'=8] {'tensor'}, dimensions={1}, use_global_device_ids=true | all-gather | bytes 147456 | tf_op jit(solution)/shard_map/all_gather | solution.py:30
  60.5 12.0 %all-to-all-start.1 = ((bf16[64,6,2048]{2,1,0:T(8,128)(2,1)}), bf16[64,6,2048]{2,1,0:T(8,128)(2,1)}, u32[]{:S(2)}, u32[]{:S(2)}) async-start(bf16[64,6,2048]{2,1,0:T(8,128)(2,1)} %reshape.153), calls=%async_computation.1 | async-start | bytes 4194304 | tf_op jit(solution)/shard_map/all_to_all | solution.py:40
  72.5 19.7 %all_gather.7 = bf16[32,2048]{1,0:T(8,128)(2,1)S(1)} all-gather(bf16[32,256]{1,0:T(8,128)(2,1)S(1)} %copy-done.6), channel_id=1, replica_groups=mesh['dp'=2,'expert'=64,'tensor'=8] {'tensor'}, dimensions={1}, use_global_device_ids=true | all-gather | bytes 147456 | tf_op jit(solution)/shard_map/all_gather | solution.py:31
  94.4 21.1 %all-to-all-done.1 = bf16[64,6,2048]{2,1,0:T(8,128)(2,1)} async-done(((bf16[64,6,2048]{2,1,0:T(8,128)(2,1)}), bf16[64,6,2048]{2,1,0:T(8,128)(2,1)}, u32[]{:S(2)}, u32[]{:S(2)}) %all-to-all-start.1) | async-done | bytes 1572896 | tf_op jit(solution)/shard_map/all_to_all | solution.py:40
  115.5 18.0 %all-to-all-start.3 = ((bf16[64,6,2048]{2,1,0:T(8,128)(2,1)}), bf16[64,6,2048]{2,1,0:T(8,128)(2,1)S(1)}, u32[]{:S(2)}, u32[]{:S(2)}) async-start(bf16[64,6,2048]{2,1,0:T(8,128)(2,1)} %reshape.160), calls=%async_computation.4 | async-start | bytes 4194304 | tf_op jit(solution)/shard_map/all_to_all | solution.py:41
  133.9 4.4 %convolution_bitcast_fusion.4 = f32[64,1,6,256]{3,0,2,1:T(8,128)} fusion(bf16[1,2048,256]{2,1,0:T(8,128)(2,1)} %param.11, bf16[64,6,2048]{2,1,0:T(8,128)(2,1)} %all-to-all-done.1), kind=kOutput, calls=%fused_computation.10 | convolution fusion | flops 402653184 | bytes 3014656 | tf_op jit(solution)/shard_map/sxcl,xlh->sxch/dot_general | solution.py:55
  138.3 43.9 %all-to-all-done.3 = bf16[64,6,2048]{2,1,0:T(8,128)(2,1)S(1)} async-done(((bf16[64,6,2048]{2,1,0:T(8,128)(2,1)}), bf16[64,6,2048]{2,1,0:T(8,128)(2,1)S(1)}, u32[]{:S(2)}, u32[]{:S(2)}) %all-to-all-start.3) | async-done | bytes 1572896 | tf_op jit(solution)/shard_map/all_to_all | solution.py:41
  182.2 3.3 convolution_bitcast_fusion.3
  185.6 4.3 %fusion.14 = (bf16[64,6,256]{2,0,1:T(8,128)(2,1)}, bf16[64,1,6,256]{3,0,2,1:T(8,128)(2,1)S(1)}, bf16[64,6,256]{2,0,1:T(8,128)(2,1)S(1)}) fusion(f32[64,1,6,256]{3,0,2,1:T(8,128)S(1)} %convolution_bitcast_fusion.3, f32[64,1,6,256]{3,0,2,1:T(8,128)S(1)} %copy-done.7, bf16[1,2048,256]{2,1,0:T(8,128)(2,1)S(1)} %copy-done, bf16[64,6,2048]{2,1,0:T(8,128)(2,1)} %all-to-all-done.1), kind=kOutput, calls=%fused_computation.36 | convolution fusion | flops 404127744 | bytes 3997696 | tf_op jit(solution)/shard_map/sxcl,xlh->sxch/dot_general | solution.py:54
  190.5 2.2 fusion
  194.1 2.3 add_bitcast_fusion
  196.5 4.3 %convolution_bitcast_fusion = f32[1,256,2048]{2,1,0:T(8,128)} fusion(bf16[64,6,256]{2,0,1:T(8,128)(2,1)} %copy-done.3, bf16[64,6,2048]{2,1,0:T(8,128)(2,1)S(1)} %all-to-all-done.3, f32[64,6]{0,1:T(8,128)S(1)} %copy.78), kind=kOutput, calls=%fused_computation.6 | convolution fusion | flops 405012480 | bytes 3868160 | tf_op jit(solution)/shard_map/sxch,sxcl->xhl/dot_general | solution.py:93
  200.9 4.3 %convolution_bitcast_fusion.2 = f32[1,2048,256]{2,1,0:T(8,128)} fusion(bf16[64,6,2048]{2,1,0:T(8,128)(2,1)} %all-to-all-done.1, bf16[64,1,6,256]{3,0,2,1:T(8,128)(2,1)S(1)} %get-tuple-element.6), kind=kOutput, calls=%fused_computation.8 | convolution fusion | flops 402653184 | bytes 3866624 | tf_op jit(solution)/shard_map/sxcl,sxch->xlh/dot_general | solution.py:89
  206.1 4.2 %convolution_bitcast_fusion.1 = f32[1,2048,256]{2,1,0:T(8,128)} fusion(bf16[64,6,256]{2,0,1:T(8,128)(2,1)S(1)} %copy-done.5, bf16[64,6,2048]{2,1,0:T(8,128)(2,1)} %all-to-all-done.1), kind=kOutput, calls=%fused_computation.7 | convolution fusion | flops 402653184 | bytes 3866624 | tf_op jit(solution)/shard_map/sxcl,sxch->xlh/dot_general | solution.py:92
  210.3 29.9 %reduce-scatter.6.cloned.1.call-done = f32[64,1,6,256]{3,0,2,1:T(8,128)} async-done(((f32[64,1,6,2048]{3,0,2,1:T(8,128)}), f32[64,1,6,256]{3,0,2,1:T(8,128)}) %reduce-scatter.6.cloned.1.call-update) | async-done | bytes 393232 | tf_op jit(solution)/shard_map/reduce_scatter | solution.py:72
  242.0 13.3 %all-to-all-start.2 = ((bf16[64,6,256]{2,1,0:T(8,128)(2,1)}), bf16[64,6,256]{2,1,0:T(8,128)(2,1)S(1)}, u32[]{:S(2)}, u32[]{:S(2)}) async-start(bf16[64,6,256]{2,1,0:T(8,128)(2,1)} %copy.81), calls=%async_computation.3 | async-start | bytes 524288 | tf_op jit(solution)/shard_map/all_to_all | solution.py:80
  255.4 40.4 %reduce-scatter.8.cloned.1.call-done = f32[64,1,6,256]{3,0,2,1:T(8,128)} async-done(((f32[64,1,6,2048]{3,0,2,1:T(8,128)}), f32[64,1,6,256]{3,0,2,1:T(8,128)}) %reduce-scatter.8.cloned.1.call-update) | async-done | bytes 393232 | tf_op jit(solution)/shard_map/reduce_scatter | solution.py:73
  297.6 13.3 %all-to-all-start.4 = ((bf16[64,6,256]{2,1,0:T(8,128)(2,1)}), bf16[64,6,256]{2,1,0:T(8,128)(2,1)S(1)}, u32[]{:S(2)}, u32[]{:S(2)}) async-start(bf16[64,6,256]{2,1,0:T(8,128)(2,1)} %copy.84), calls=%async_computation.6 | async-start | bytes 524288 | tf_op jit(solution)/shard_map/all_to_all | solution.py:81
  311.0 14.2 %reduce-scatter.14.cloned.1.call-done = f32[1,256,1024]{2,1,0:T(8,128)} async-done(((f32[1,256,2048]{2,1,0:T(8,128)}), f32[1,256,1024]{2,1,0:T(8,128)}) %reduce-scatter.14.cloned.1.call-update) | async-done | bytes 1048592 | tf_op jit(solution)/shard_map/reduce_scatter | solution.py:97
  325.2 2.1 convert_element_type.117
  327.3 23.9 %reduce-scatter.10.cloned.1.call-done = f32[1,1024,256]{2,1,0:T(8,128)} async-done(((f32[1,2048,256]{2,1,0:T(8,128)}), f32[1,1024,256]{2,1,0:T(8,128)}) %reduce-scatter.10.cloned.1.call-update) | async-done | bytes 1048592 | tf_op jit(solution)/shard_map/reduce_scatter | solution.py:95
  353.2 23.5 %reduce-scatter.12.cloned.1.call-done = f32[1,1024,256]{2,1,0:T(8,128)} async-done(((f32[1,2048,256]{2,1,0:T(8,128)}), f32[1,1024,256]{2,1,0:T(8,128)}) %reduce-scatter.12.cloned.1.call-update) | async-done | bytes 1048592 | tf_op jit(solution)/shard_map/reduce_scatter | solution.py:96
  (63 shorter events, 21.3 us)
Async XLA Ops:
  7.2 178.4 %copy-start = (bf16[1,2048,256]{2,1,0:T(8,128)(2,1)S(1)}, bf16[1,2048,256]{2,1,0:T(8,128)(2,1)}, u32[]{:S(2)}) copy-start(bf16[1,2048,256]{2,1,0:T(8,128)(2,1)} %param.10) | copy-start | bytes 3145732
  11.0 49.5 %all-to-all-start = ((bf16[64,1,6]{2,1,0:T(2,128)(2,1)}), bf16[64,1,6]{2,1,0:T(2,128)(2,1)S(1)}, u32[]{:S(2)}, u32[]{:S(2)}) async-start(bf16[64,1,6]{2,1,0:T(2,128)(2,1)} %convert_element_type.120), calls=%async_computation | async-start | bytes 65536 | tf_op jit(solution)/shard_map/all_to_all | solution.py:42
  60.5 12.0 %copy-start.6 = (bf16[32,256]{1,0:T(8,128)(2,1)S(1)}, bf16[32,256]{1,0:T(8,128)(2,1)}, u32[]{:S(2)}) copy-start(bf16[32,256]{1,0:T(8,128)(2,1)} %param.15) | copy-start | bytes 49156
  60.5 55.0 %all-to-all-start.1 = ((bf16[64,6,2048]{2,1,0:T(8,128)(2,1)}), bf16[64,6,2048]{2,1,0:T(8,128)(2,1)}, u32[]{:S(2)}, u32[]{:S(2)}) async-start(bf16[64,6,2048]{2,1,0:T(8,128)(2,1)} %reshape.153), calls=%async_computation.1 | async-start | bytes 4194304 | tf_op jit(solution)/shard_map/all_to_all | solution.py:40
  115.5 66.7 %all-to-all-start.3 = ((bf16[64,6,2048]{2,1,0:T(8,128)(2,1)}), bf16[64,6,2048]{2,1,0:T(8,128)(2,1)S(1)}, u32[]{:S(2)}, u32[]{:S(2)}) async-start(bf16[64,6,2048]{2,1,0:T(8,128)(2,1)} %reshape.160), calls=%async_computation.4 | async-start | bytes 4194304 | tf_op jit(solution)/shard_map/all_to_all | solution.py:41
  133.5 106.6 %reduce-scatter.6.cloned.1.call-start = ((), (), s32[]{:S(2)}) async-start(), calls=%async_computation.10 | async-start | bytes 3538944 | tf_op jit(solution)/shard_map/reduce_scatter | solution.py:72
  182.2 3.4 copy-start.7
  185.6 5.0 %copy-start.1 = (bf16[1,256,2048]{2,1,0:T(8,128)(2,1)S(1)}, bf16[1,256,2048]{2,1,0:T(8,128)(2,1)}, u32[]{:S(2)}) copy-start(bf16[1,256,2048]{2,1,0:T(8,128)(2,1)} %param.12) | copy-start | bytes 3145732
  189.9 0.7 copy-start.3
  192.8 103.0 %reduce-scatter.8.cloned.1.call-start = ((), (), s32[]{:S(2)}) async-start(), calls=%async_computation.11 | async-start | bytes 3538944 | tf_op jit(solution)/shard_map/reduce_scatter | solution.py:73
  192.8 1.2 copy-start.2
  192.9 1.2 copy-start.4
  196.4 128.8 %reduce-scatter.14.cloned.1.call-start = ((), (), s32[]{:S(2)}) async-start(), calls=%async_computation.14 | async-start | bytes 3145728 | tf_op jit(solution)/shard_map/reduce_scatter | solution.py:97
  200.8 150.3 %reduce-scatter.10.cloned.1.call-start = ((), (), s32[]{:S(2)}) async-start(), calls=%async_computation.12 | async-start | bytes 3145728 | tf_op jit(solution)/shard_map/reduce_scatter | solution.py:95
  205.1 0.9 copy-start.5
  205.2 171.5 %reduce-scatter.12.cloned.1.call-start = ((), (), s32[]{:S(2)}) async-start(), calls=%async_computation.13 | async-start | bytes 3145728 | tf_op jit(solution)/shard_map/reduce_scatter | solution.py:96
  242.0 55.6 %all-to-all-start.2 = ((bf16[64,6,256]{2,1,0:T(8,128)(2,1)}), bf16[64,6,256]{2,1,0:T(8,128)(2,1)S(1)}, u32[]{:S(2)}, u32[]{:S(2)}) async-start(bf16[64,6,256]{2,1,0:T(8,128)(2,1)} %copy.81), calls=%async_computation.3 | async-start | bytes 524288 | tf_op jit(solution)/shard_map/all_to_all | solution.py:80
  297.6 81.9 %all-to-all-start.4 = ((bf16[64,6,256]{2,1,0:T(8,128)(2,1)}), bf16[64,6,256]{2,1,0:T(8,128)(2,1)S(1)}, u32[]{:S(2)}, u32[]{:S(2)}) async-start(bf16[64,6,256]{2,1,0:T(8,128)(2,1)} %copy.84), calls=%async_computation.6 | async-start | bytes 524288 | tf_op jit(solution)/shard_map/all_to_all | solution.py:81
Sparse Core Ops, SparseCore 0:
  192.9 47.2 reduce-scatter.5
  243.6 52.1 reduce-scatter.7
  299.2 25.9 reduce-scatter.13
  328.8 22.3 reduce-scatter.9
  354.3 22.2 reduce-scatter.11
where the time goes:
time: 388 us; the launch traced here: 387 us
  waiting for transfers between devices  197 us (51%)
  starting transfers between devices  81.3 us (21%)
  blocking collectives  39.5 us (10%)
  matrix products  35.8 us (9%)
  between operations  14 us (4%)
  local copies, waits for them, and re-layouts  9.91 us (3%)
  other arithmetic  9.43 us (2%)
    all_to_all x1, waiting for transfers between devices, per_device(): lax.all_to_all(to_slots(source_cot), 'expert', split_axis=0, concat_axis=...  43.9 us
    reduce_scatter x1, waiting for transfers between devices, per_device(): lax.psum_scatter(partial_back, 'tensor', scatter_dimension=3, tiled=True)  40.4 us
    reduce_scatter x1, waiting for transfers between devices, per_device(): lax.psum_scatter(partial_out, 'tensor', scatter_dimension=3, tiled=True)  29.9 us
    all_to_all x1, starting transfers between devices, per_device(): lax.all_to_all(gate_slot.reshape(groups, held_experts * capacity), 'exper...  24 us
    reduce_scatter x1, waiting for transfers between devices, per_device(): lax.psum_scatter(wide_gate, 'dp', scatter_dimension=1, tiled=True)  23.9 us
    reduce_scatter x1, waiting for transfers between devices, per_device(): lax.psum_scatter(wide_up, 'dp', scatter_dimension=1, tiled=True)  23.5 us
    all_to_all x1, waiting for transfers between devices, per_device(): lax.all_to_all(to_slots(source_rows), 'expert', split_axis=0, concat_axis...  21.1 us
    all_gather x1, blocking collectives, per_device(): lax.all_gather(latent_cols, 'tensor', axis=1, tiled=True)  19.9 us
  transfers between devices with their start and end apart: 10, of which 7 were waited for; matrix products, arithmetic and copies ran while one was open for 10% of the time, Pallas kernels for 0%

commit v1 on v0

v1 whole, which is shorter than its diff:
```python
import functools

import jax
import jax.numpy as jnp
from jax import lax
from jax.experimental import pallas as pl
from jax.experimental.pallas import tpu as pltpu
from jax.sharding import PartitionSpec as P

F32 = jnp.float32
BF16 = jnp.bfloat16
MESH = pl.DeviceIdType.MESH
CAP = 6
PAD = 8
R, L_ = 0, 1
OUT, BACK = 0, 1


def dot(a, b, contract):
    return lax.dot_general(a, b, (contract, ((), ())), preferred_element_type=F32)


NN = ((1,), (0,))
NT = ((1,), (1,))
TN = ((0,), (0,))


def slot_maps(ids, gates, groups):
    tok, top = ids.shape
    lane = lax.broadcasted_iota(jnp.int32, (tok, groups), 1)
    member = jnp.zeros((tok, groups), F32)
    weight = jnp.zeros((tok, groups), F32)
    for k in range(top):
        hit = ids[:, k : k + 1] == lane
        member = member + jnp.where(hit, 1.0, 0.0)
        weight = weight + jnp.where(hit, gates[:, k : k + 1].astype(F32), 0.0)
    earlier = lax.broadcasted_iota(jnp.int32, (tok, tok), 0) > lax.broadcasted_iota(
        jnp.int32, (tok, tok), 1
    )
    place = dot(jnp.where(earlier, 1.0, 0.0).astype(BF16), member.astype(BF16), NN)
    cols = groups * 2 * PAD
    widen = jnp.where(
        lax.shift_right_logical(lax.broadcasted_iota(jnp.int32, (groups, cols), 1), 4)
        == lax.broadcasted_iota(jnp.int32, (groups, cols), 0),
        1.0,
        0.0,
    ).astype(BF16)
    col = lax.broadcasted_iota(jnp.int32, (tok, cols), 1)
    slot = lax.bitwise_and(col, PAD - 1).astype(F32)
    part = lax.bitwise_and(col, PAD)
    here = jnp.where(
        dot(place.astype(BF16), widen, NN) == slot, dot(member.astype(BF16), widen, NN), 0.0
    )
    scaled = here * dot(weight.astype(BF16), widen, NN)
    return here, scaled, part == 0


def kernel(
    sizes,
    tokens,
    w_latent,
    w_gate,
    w_up,
    w_out,
    ids,
    gates,
    cot,
    latent_out,
    latent_grad,
    grad_gate,
    grad_up,
    grad_out,
    tok_v,
    wl_v,
    wgu,
    wo,
    comb,
    disp,
    land,
    ag,
    acc_h,
    acc_a,
    act,
    act_t,
    gug,
    rs_send,
    rs_recv,
    fin,
    ret,
    home,
    dp_gu_send,
    dp_gu_recv,
    dp_o_send,
    dp_o_recv,
    stage_gu,
    stage_o,
    load_sem,
    lat_sem,
    own_sem,
    a2a_send,
    a2a_recv,
    ag_send,
    ag_recv,
    rs_ssem,
    rs_rsem,
    dp_ssem,
    dp_rsem,
    store_sem,
):
    groups, ring, lat_steps, batch = sizes
    half = ring // 2
    wide = cot.shape[1]
    hid = wo.shape[1]
    rows = groups * CAP
    batches = groups // batch
    brow = batch * CAP
    tok = cot.shape[0]
    me_d, me_e, me_x = lax.axis_index("dp"), lax.axis_index("expert"), lax.axis_index("tensor")
    peer_d = 1 - me_d
    toward = (lax.rem(me_x + 1, ring), lax.rem(me_x + ring - 1, ring))

    barrier = pltpu.get_barrier_semaphore()

    @pl.loop(1, groups)
    def _(i):
        pl.semaphore_signal(
            barrier, 1, device_id={"expert": lax.rem(me_e + i, groups)}, device_id_type=MESH
        )

    for there in toward:
        pl.semaphore_signal(barrier, 1, device_id={"tensor": there}, device_id_type=MESH)
    pl.semaphore_signal(barrier, 1, device_id={"dp": peer_d}, device_id_type=MESH)

    depth = wl_v.shape[1]
    lat_copies = []
    for i in range(lat_steps):
        lat_copies.append(
            (
                pltpu.make_async_copy(
                    tokens.at[:, pl.ds(i * depth, depth)], tok_v.at[i], lat_sem.at[0, i]
                ),
                pltpu.make_async_copy(
                    w_latent.at[pl.ds(i * depth, depth), :], wl_v.at[i], lat_sem.at[1, i]
                ),
            )
        )
    for pair in lat_copies:
        for copy in pair:
            copy.start()
    weight_copies = []
    for i in range(ring):
        for which, copy_of in enumerate(
            (
                (w_gate.at[0, pl.ds(i * wide, wide), :], wgu.at[i, :, pl.ds(0, hid)]),
                (w_up.at[0, pl.ds(i * wide, wide), :], wgu.at[i, :, pl.ds(hid, hid)]),
                (w_out.at[0, :, pl.ds(i * wide, wide)], wo.at[i]),
            )
        ):
            copy = pltpu.make_async_copy(*copy_of, load_sem.at[which, i])
            copy.start()
            weight_copies.append(copy)

    here, scaled, forward = slot_maps(ids[...], gates[...], groups)
    comb[0] = jnp.where(forward, scaled, 0.0).astype(BF16)
    comb[1] = jnp.where(forward, 0.0, here).astype(BF16)
    to_rows = jnp.where(forward, here, 0.0).astype(BF16)
    to_cot = jnp.where(forward, 0.0, scaled).astype(BF16)
    latent = jnp.zeros((tok, wide), F32)
    for i, pair in enumerate(lat_copies):
        for copy in pair:
            copy.wait()
        latent = latent + dot(tok_v[i], wl_v[i], NN)
    disp[...] = (
        (dot(to_rows, latent.astype(BF16), TN) + dot(to_cot, cot[...], TN))
        .astype(BF16)
        .reshape(disp.shape)
    )
    pl.semaphore_wait(barrier, groups + 2)

    def exchange(src, dst, which):
        @pl.loop(1, groups)
        def _(i):
            there = lax.rem(me_e + i, groups)
            pltpu.make_async_remote_copy(
                src_ref=src.at[there],
                dst_ref=dst.at[me_e],
                send_sem=a2a_send.at[which],
                recv_sem=a2a_recv.at[which],
                device_id={"expert": there},
                device_id_type=MESH,
            ).start()

        own = pltpu.make_async_copy(src.at[me_e], dst.at[me_e], own_sem.at[which])
        own.start()
        own.wait()
        some = pl.ds(0, groups - 1)
        return pltpu.make_async_remote_copy(
            src_ref=src.at[some],
            dst_ref=dst.at[some],
            send_sem=a2a_send.at[which],
            recv_sem=a2a_recv.at[which],
            device_id={"expert": lax.rem(me_e + 1, groups)},
            device_id_type=MESH,
        )

    dispatch = exchange(disp, land, 0)

    def picks(shape, row_dim):
        col = lax.broadcasted_iota(jnp.int32, shape, 1 - row_dim)
        row = lax.broadcasted_iota(jnp.int32, shape, row_dim)
        slot = lax.bitwise_and(col, PAD - 1)
        part = lax.bitwise_and(lax.shift_right_logical(col, 3), 1)
        want = part * brow + lax.shift_right_logical(col, 4) * CAP + slot
        return jnp.where((row == want) & (slot < CAP), 1.0, 0.0).astype(BF16)

    block = batch * 2 * PAD
    squeeze = picks((2 * brow, block), 0)
    dispatch.wait_recv()
    for b in range(batches):
        packed = dot(squeeze, land[b * batch : (b + 1) * batch].reshape(block, wide), NN)
        packed = packed.astype(BF16)
        ag[me_x, OUT, pl.ds(b * brow, brow), :] = packed[:brow]
        ag[me_x, BACK, pl.ds(b * brow, brow), :] = packed[brow:]

    def ag_copy(way, part, step):
        back = step - 1
        owner = lax.rem(me_x + (ring - back if way == R else back), ring)
        return pltpu.make_async_remote_copy(
            src_ref=ag.at[owner, part],
            dst_ref=ag.at[owner, part],
            send_sem=ag_send.at[way, part, back],
            recv_sem=ag_recv.at[way, part, back],
            device_id={"tensor": toward[way]},
            device_id_type=MESH,
        )

    streams = ((R, OUT), (L_, BACK), (R, BACK), (L_, OUT))

    def last_of(way, part):
        return half if (way == R) == (part == OUT) else half - 1

    ag_copies = {
        (way, part, step): ag_copy(way, part, step)
        for way, part in streams
        for step in range(1, last_of(way, part) + 1)
    }
    for way, part in streams:
        if last_of(way, part) >= 1:
            ag_copies[way, part, 1].start()

    for copy in weight_copies:
        copy.wait()

    def absorb(owner, first=False):
        h = dot(ag[owner, OUT], wgu[owner], NN)
        a = dot(ag[owner, BACK], wo[owner], NT)
        if first:
            acc_h[...] = h
            acc_a[...] = a
        else:
            acc_h[...] += h
            acc_a[...] += a

    absorb(me_x, first=True)
    for step in range(1, half + 1):
        for way, part in streams:
            if step <= last_of(way, part):
                ag_copies[way, part, step].wait_recv()
                if step < last_of(way, part):
                    ag_copies[way, part, step + 1].start()
        absorb(lax.rem(me_x + ring - step, ring))
        if step < half:
            absorb(lax.rem(me_x + step, ring))

    pre_gate, pre_up, act_grad = acc_h[:, :hid], acc_h[:, hid:], acc_a[...]
    sig = jax.nn.sigmoid(pre_gate)
    silu = pre_gate * sig
    activated = silu * pre_up
    act[...] = activated.astype(BF16)
    gug[:, :hid] = (act_grad * pre_up * sig * (1.0 + pre_gate * (1.0 - sig))).astype(BF16)
    gug[:, hid:] = (act_grad * silu).astype(BF16)

    def contribution(part, owner):
        if part == OUT:
            return dot(act[...], wo[owner], NN)
        return dot(gug[...], wgu[owner], NT)

    def rs_copy(way, part, step):
        return pltpu.make_async_remote_copy(
            src_ref=rs_send.at[way, part, step - 1],
            dst_ref=rs_recv.at[way, part, step - 1],
            send_sem=rs_ssem.at[way, part, step - 1],
            recv_sem=rs_rsem.at[way, part, step - 1],
            device_id={"tensor": toward[way]},
            device_id_type=MESH,
        )

    rs_copies = {}

    def push(way, part, step):
        ahead = half + 1 - step
        owner = lax.rem(me_x + (ahead if way == R else ring - ahead), ring)
        value = contribution(part, owner)
        if (way, part, step - 1) in rs_copies:
            rs_copies[way, part, step - 1].wait_recv()
            value = value + rs_recv[way, part, step - 2].astype(F32)
        rs_send[way, part, step - 1] = value.astype(BF16)
        rs_copies[way, part, step] = rs_copy(way, part, step)
        rs_copies[way, part, step].start()

    push(R, OUT, 1)
    push(L_, BACK, 1)
    if half > 1:
        push(R, BACK, 2)
        push(L_, OUT, 2)

    act_t[...] = act[...].T
    dp_copies = []

    def grads_of(owner):
        return dot(ag[owner, OUT], gug[...], TN), dot(act_t[...], ag[owner, BACK], NN)

    def for_peer(i):
        gu, o = grads_of(peer_d * half + i)
        dp_gu_send[i] = gu.astype(BF16)
        dp_o_send[i] = o.astype(BF16)
        for j, (src, dst) in enumerate(((dp_gu_send, dp_gu_recv), (dp_o_send, dp_o_recv))):
            copy = pltpu.make_async_remote_copy(
                src_ref=src.at[i],
                dst_ref=dst.at[i],
                send_sem=dp_ssem.at[j, i],
                recv_sem=dp_rsem.at[j, i],
                device_id={"dp": peer_d},
                device_id_type=MESH,
            )
            copy.start()
            dp_copies.append(copy)

    stores = []

    def for_self(i):
        gu, o = grads_of(me_d * half + i)
        for copy in dp_copies[2 * i : 2 * i + 2]:
            copy.wait_recv()
        stage_gu[i] = (gu + dp_gu_recv[i].astype(F32)).astype(BF16)
        stage_o[i] = (o + dp_o_recv[i].astype(F32)).astype(BF16)
        for j, (src, dst) in enumerate(
            (
                (stage_gu.at[i, :, pl.ds(0, hid)], grad_gate.at[0, pl.ds(i * wide, wide), :]),
                (stage_gu.at[i, :, pl.ds(hid, hid)], grad_up.at[0, pl.ds(i * wide, wide), :]),
                (stage_o.at[i], grad_out.at[0, :, pl.ds(i * wide, wide)]),
            )
        ):
            copy = pltpu.make_async_copy(src, dst, store_sem.at[j, i])
            copy.start()
            stores.append(copy)

    tasks = [functools.partial(for_peer, i) for i in range(half)]
    tasks += [functools.partial(for_self, i) for i in range(half)]
    per_step = -(-len(tasks) // max(1, half - 1))
    for step in range(2, half + 1):
        for task in tasks[:per_step]:
            task()
        tasks = tasks[per_step:]
        push(R, OUT, step)
        push(L_, BACK, step)
        if step < half:
            push(R, BACK, step + 1)
            push(L_, OUT, step + 1)
    for task in tasks:
        task()

    for part in (OUT, BACK):
        total = contribution(part, me_x)
        for way in (R, L_):
            if (way, part, half) in rs_copies:
                rs_copies[way, part, half].wait_recv()
                total = total + rs_recv[way, part, half - 1].astype(F32)
        total = total.astype(BF16)
        for b in range(batches):
            fin[b, pl.ds(part * brow, brow), :] = total[b * brow : (b + 1) * brow]

    stretch = picks((block, 2 * brow), 1)
    for b in range(batches):
        spread = dot(stretch, fin[b], NN).astype(BF16)
        ret[b * batch : (b + 1) * batch] = spread.reshape(batch, 2 * PAD, wide)

    homeward = exchange(ret, home, 1)

    for copy in ag_copies.values():
        copy.wait_send()
    for copy in rs_copies.values():
        copy.wait_send()
    for copy in dp_copies:
        copy.wait_send()
    for copy in stores:
        copy.wait()
    dispatch.wait_send()

    homeward.wait_recv()
    back = home[...].reshape(groups * 2 * PAD, wide)
    latent_out[...] = dot(comb[0], back, NN).astype(BF16)
    latent_grad[...] = dot(comb[1], back, NN).astype(BF16)
    homeward.wait_send()


def per_device(tokens, w_latent, w_gate, w_up, w_out, expert_ids, gates, cotangent):
    groups, ring = lax.axis_size("expert"), lax.axis_size("tensor")
    half = ring // 2
    tok, width = tokens.shape
    wide = cotangent.shape[1]
    hid = w_gate.shape[2]
    rows = groups * CAP
    batch = min(16, groups)
    lat_steps = 8
    depth = width // lat_steps
    dma = pltpu.SemaphoreType.DMA
    vmem = pl.BlockSpec(memory_space=pltpu.VMEM)
    hbm = pl.BlockSpec(memory_space=pl.ANY)
    flops = 2 * tok * width * wide + 18 * rows * ring * wide * hid
    return pl.pallas_call(
        functools.partial(kernel, (groups, ring, lat_steps, batch)),
        out_shape=(
            jax.ShapeDtypeStruct((tok, wide), BF16),
            jax.ShapeDtypeStruct((tok, wide), BF16),
            jax.ShapeDtypeStruct((1, half * wide, hid), BF16),
            jax.ShapeDtypeStruct((1, half * wide, hid), BF16),
            jax.ShapeDtypeStruct((1, hid, half * wide), BF16),
        ),
        in_specs=[hbm] * 5 + [vmem] * 3,
        out_specs=(vmem, vmem, hbm, hbm, hbm),
        scratch_shapes=[
            pltpu.VMEM((lat_steps, tok, depth), BF16),
            pltpu.VMEM((lat_steps, depth, wide), BF16),
            pltpu.VMEM((ring, wide, 2 * hid), BF16),
            pltpu.VMEM((ring, hid, wide), BF16),
            pltpu.VMEM((2, tok, groups * 2 * PAD), BF16),
            pltpu.VMEM((groups, 2 * PAD, wide), BF16),
            pltpu.VMEM((groups, 2 * PAD, wide), BF16),
            pltpu.VMEM((ring, 2, rows, wide), BF16),
            pltpu.VMEM((rows, 2 * hid), F32),
            pltpu.VMEM((rows, hid), F32),
            pltpu.VMEM((rows, hid), BF16),
            pltpu.VMEM((hid, rows), BF16),
            pltpu.VMEM((rows, 2 * hid), BF16),
            pltpu.VMEM((2, 2, half, rows, wide), BF16),
            pltpu.VMEM((2, 2, half, rows, wide), BF16),
            pltpu.VMEM((groups // batch, 2 * batch * CAP, wide), BF16),
            pltpu.VMEM((groups, 2 * PAD, wide), BF16),
            pltpu.VMEM((groups, 2 * PAD, wide), BF16),
            pltpu.VMEM((half, wide, 2 * hid), BF16),
            pltpu.VMEM((half, wide, 2 * hid), BF16),
            pltpu.VMEM((half, hid, wide), BF16),
            pltpu.VMEM((half, hid, wide), BF16),
            pltpu.VMEM((half, wide, 2 * hid), BF16),
            pltpu.VMEM((half, hid, wide), BF16),
            dma((3, ring)),
            dma((2, lat_steps)),
            dma((2,)),
            dma((2,)),
            dma((2,)),
            dma((2, 2, half)),
            dma((2, 2, half)),
            dma((2, 2, half)),
            dma((2, 2, half)),
            dma((2, half)),
            dma((2, half)),
            dma((3, half)),
        ],
        compiler_params=pltpu.CompilerParams(
            collective_id=0, has_side_effects=True, vmem_limit_bytes=56 * 1024 * 1024
        ),
        cost_estimate=pl.CostEstimate(
            flops=flops, bytes_accessed=10 * 1024 * 1024, transcendentals=rows * hid
        ),
    )(tokens, w_latent, w_gate, w_up, w_out, expert_ids, gates, cotangent)


def solution(mesh):
    in_specs = (
        P(("dp", "expert"), None),
        P(None, "tensor"),
        P("expert", None, "tensor"),
        P("expert", None, "tensor"),
        P("expert", "tensor", None),
        P(("dp", "expert"), None),
        P(("dp", "expert"), None),
        P(("dp", "expert"), "tensor"),
    )
    out_specs = (
        P(("dp", "expert"), "tensor"),
        P(("dp", "expert"), "tensor"),
        P("expert", "dp", "tensor"),
        P("expert", "dp", "tensor"),
        P("expert", "tensor", "dp"),
    )
    return jax.shard_map(
        per_device, mesh=mesh, in_specs=in_specs, out_specs=out_specs, check_vma=False
    )
```

time: 388 us -> 129 us (0.33)
  the two profiles are of different devices: /device:TPU:1 before, /device:TPU:4 now
where the time goes in v1:
time: 129 us
  Pallas kernels  117 us (91%)
  local copies, waits for them, and re-layouts  11 us (9%)
    pallas_call x1, Pallas kernels, per_device(): pl.pallas_call(functools.partial(kernel, (groups, ring, lat_steps, batch)...  117 us
    unnamed x7, local copies, waits for them, and re-layouts  11 us

profile of v1, /device:TPU:4, one launch (start us, length us, event | category | flops | bytes accessed | tf_op | source)
XLA Modules:
  0.0 129.0 jit_solution(2034692353215347346)
XLA Ops:
  0.6 1.4 %copy.14.gates = bf16[32,8]{1,0:T(8,128)(2,1)} copy(bf16[32,8]{0,1:T(8,128)(2,1)} %param.14) | data formatting | bytes 1024 | tf_op args[6]
  2.0 1.4 %copy.13.ids = s32[32,8]{1,0:T(8,128)} copy(s32[32,8]{0,1:T(8,128)} %param.13) | data formatting | bytes 2048 | tf_op args[5]
  3.4 117.3 %shard_map.119 = (bf16[32,256]{1,0:T(8,128)(2,1)}, bf16[32,256]{1,0:T(8,128)(2,1)}, bf16[1,1024,256]{2,1,0:T(8,128)(2,1)}, bf16[1,1024,256]{2,1,0:T(8,128)(2,1)}, bf16[1,256,1024]{2,1,0:T(8,128)(2,1)}) custom-call(bf16[32,8192]{1,0:T(8,128)(2,1)} %tokens.1, bf16[8192,256]{1,0:T(8,128)(2,1)} %w_latent.1, bf16[1,2048,256]{2,1,0:T(8,128)(2,1)} %w_gate.1, ...), custom_call_target="tpu_custom_call" | custom-call | flops 3758096384 | bytes 10485760 | tf_op jit(solution)/shard_map/pallas_call | solution.py:421
  120.7 1.3 %copy.20 = bf16[32,256]{1,0:T(8,128)(2,1)} copy(bf16[32,256]{1,0:T(8,128)(2,1)} %get-tuple-element.10) | data formatting | bytes 32768
  122.0 1.3 %copy.21 = bf16[32,256]{1,0:T(8,128)(2,1)} copy(bf16[32,256]{1,0:T(8,128)(2,1)} %get-tuple-element.11) | data formatting | bytes 32768
  123.4 1.9 %copy.22 = bf16[1,1024,256]{2,1,0:T(8,128)(2,1)} copy(bf16[1,1024,256]{2,1,0:T(8,128)(2,1)} %get-tuple-element.12) | data formatting | bytes 1048576
  125.2 1.9 %copy.23 = bf16[1,1024,256]{2,1,0:T(8,128)(2,1)} copy(bf16[1,1024,256]{2,1,0:T(8,128)(2,1)} %get-tuple-element.13) | data formatting | bytes 1048576
  127.1 1.9 %copy.24 = bf16[1,256,1024]{2,1,0:T(8,128)(2,1)} copy(bf16[1,256,1024]{2,1,0:T(8,128)(2,1)} %get-tuple-element.14) | data formatting | bytes 1048576

commit v2 on v1

v2 whole, which is shorter than its diff:
```python
import functools

import jax
import jax.numpy as jnp
from jax import lax
from jax.experimental import pallas as pl
from jax.experimental.pallas import tpu as pltpu
from jax.sharding import PartitionSpec as P

F32 = jnp.float32
BF16 = jnp.bfloat16
MESH = pl.DeviceIdType.MESH
CAP = 6
PAD = 8
R, L_ = 0, 1
OUT, BACK = 0, 1


def dot(a, b, contract):
    return lax.dot_general(a, b, (contract, ((), ())), preferred_element_type=F32)


NN = ((1,), (0,))
NT = ((1,), (1,))
TN = ((0,), (0,))


def slot_maps(ids, gates, groups):
    top, tok = ids.shape
    expert = lax.broadcasted_iota(jnp.int32, (groups, tok), 0)
    member = jnp.zeros((groups, tok), F32)
    weight = jnp.zeros((groups, tok), F32)
    for k in range(top):
        hit = ids[k : k + 1, :] == expert
        member = member + jnp.where(hit, 1.0, 0.0)
        weight = weight + jnp.where(hit, gates[k : k + 1, :].astype(F32), 0.0)
    earlier = lax.broadcasted_iota(jnp.int32, (tok, tok), 0) < lax.broadcasted_iota(
        jnp.int32, (tok, tok), 1
    )
    place = dot(member.astype(BF16), jnp.where(earlier, 1.0, 0.0).astype(BF16), NN)
    cols = groups * 2 * PAD
    widen = jnp.where(
        lax.shift_right_logical(lax.broadcasted_iota(jnp.int32, (groups, cols), 1), 4)
        == lax.broadcasted_iota(jnp.int32, (groups, cols), 0),
        1.0,
        0.0,
    ).astype(BF16)
    col = lax.broadcasted_iota(jnp.int32, (tok, cols), 1)
    slot = lax.bitwise_and(col, PAD - 1).astype(F32)
    part = lax.bitwise_and(col, PAD)
    here = jnp.where(
        dot(place.astype(BF16), widen, TN) == slot, dot(member.astype(BF16), widen, TN), 0.0
    )
    scaled = here * dot(weight.astype(BF16), widen, TN)
    return here, scaled, part == 0


def picks(shape, row_dim, brow):
    col = lax.broadcasted_iota(jnp.int32, shape, 1 - row_dim)
    row = lax.broadcasted_iota(jnp.int32, shape, row_dim)
    slot = lax.bitwise_and(col, PAD - 1)
    part = lax.bitwise_and(lax.shift_right_logical(col, 3), 1)
    want = part * brow + lax.shift_right_logical(col, 4) * CAP + slot
    return jnp.where((row == want) & (slot < CAP), 1.0, 0.0).astype(BF16)


def kernel(
    sizes,
    tokens,
    w_latent,
    w_gate,
    w_up,
    w_out,
    ids,
    gates,
    cot,
    latent_out,
    latent_grad,
    grad_gate,
    grad_up,
    grad_out,
    tok_v,
    wl_v,
    wgu,
    wo,
    comb,
    disp,
    land,
    ag,
    acc_h,
    acc_a,
    act,
    act_t,
    gug,
    rs_send,
    rs_recv,
    fin,
    ret,
    home,
    squeeze,
    stretch,
    dp_gu_send,
    dp_gu_recv,
    dp_o_send,
    dp_o_recv,
    stage_gu,
    stage_o,
    load_sem,
    lat_sem,
    own_sem,
    a2a_send,
    land_sem,
    home_sem,
    ag_send,
    ag_recv,
    rs_ssem,
    rs_rsem,
    dp_ssem,
    dp_rsem,
    store_sem,
):
    groups, span, ring, lat_steps = sizes
    lines = groups // span
    half = ring // 2
    wide = cot.shape[1]
    hid = wo.shape[1]
    batch, batches = 2 * span, lines // 2
    brow = batch * CAP
    rows = groups * CAP
    tok = cot.shape[0]
    block = batch * 2 * PAD
    me_d, me_e, me_x = lax.axis_index("dp"), lax.axis_index("expert"), lax.axis_index("tensor")
    peer_d = 1 - me_d
    toward = ((me_x + 1) % ring, (me_x + ring - 1) % ring)

    barrier = pltpu.get_barrier_semaphore()

    @pl.loop(1, groups)
    def _(i):
        pl.semaphore_signal(
            barrier, 1, device_id={"expert": (me_e + i) % groups}, device_id_type=MESH
        )

    for there in toward:
        pl.semaphore_signal(barrier, 1, device_id={"tensor": there}, device_id_type=MESH)
    pl.semaphore_signal(barrier, 1, device_id={"dp": peer_d}, device_id_type=MESH)

    depth = wl_v.shape[1]
    lat_copies = []
    for i in range(lat_steps):
        lat_copies.append(
            (
                pltpu.make_async_copy(
                    tokens.at[:, pl.ds(i * depth, depth)], tok_v.at[i], lat_sem.at[0, i]
                ),
                pltpu.make_async_copy(
                    w_latent.at[pl.ds(i * depth, depth), :], wl_v.at[i], lat_sem.at[1, i]
                ),
            )
        )
    for pair in lat_copies:
        for copy in pair:
            copy.start()
    weight_copies = []
    for i in range(ring):
        for which, copy_of in enumerate(
            (
                (w_gate.at[0, pl.ds(i * wide, wide), :], wgu.at[i, :, pl.ds(0, hid)]),
                (w_up.at[0, pl.ds(i * wide, wide), :], wgu.at[i, :, pl.ds(hid, hid)]),
                (w_out.at[0, :, pl.ds(i * wide, wide)], wo.at[i]),
            )
        ):
            copy = pltpu.make_async_copy(*copy_of, load_sem.at[which, i])
            copy.start()
            weight_copies.append(copy)

    here, scaled, forward = slot_maps(ids[...], gates[...], groups)
    comb[0] = jnp.where(forward, scaled, 0.0).astype(BF16)
    comb[1] = jnp.where(forward, 0.0, here).astype(BF16)
    to_rows = jnp.where(forward, here, 0.0).astype(BF16)
    to_cot = jnp.where(forward, 0.0, scaled).astype(BF16)
    latent = jnp.zeros((tok, wide), F32)
    for i, pair in enumerate(lat_copies):
        for copy in pair:
            copy.wait()
        latent = latent + dot(tok_v[i], wl_v[i], NN)
    disp[...] = (
        (dot(to_rows, latent.astype(BF16), TN) + dot(to_cot, cot[...], TN))
        .astype(BF16)
        .reshape(disp.shape)
    )
    squeeze[...] = picks((2 * brow, block), 0, brow)
    stretch[...] = picks((block, 2 * brow), 1, brow)
    pl.semaphore_wait(barrier, groups + 2)

    me_line, me_place = me_e // span, me_e % span

    def other(p, q, sign):
        odd, line_odd = (q // 2) % 2, q % 2
        by = q // 4
        d_place = by + odd * (span - 1 - 2 * by)
        d_line = p + line_odd * (lines - 1 - 2 * p)
        if sign < 0:
            d_place, d_line = span - d_place, lines - d_line
        return ((me_line + d_line) % lines) * span + (me_place + d_place) % span

    def dispatch_copy(p, q):
        there = other(p, q, 1)
        return pltpu.make_async_remote_copy(
            src_ref=disp.at[there],
            dst_ref=land.at[p * batch + q],
            send_sem=a2a_send.at[0],
            recv_sem=land_sem.at[p],
            device_id={"expert": there},
            device_id_type=MESH,
        )

    own = pltpu.make_async_copy(disp.at[me_e], land.at[0], own_sem.at[0])
    own.start()
    for p in range(batches):

        @pl.loop(1 if p == 0 else 0, batch)
        def _(q, p=p):
            dispatch_copy(p, q).start()

    def many(buffer, first, count, send_sem, recv_sem):
        part = buffer.at[pl.ds(first, count)]
        return pltpu.make_async_remote_copy(
            src_ref=part,
            dst_ref=part,
            send_sem=send_sem,
            recv_sem=recv_sem,
            device_id={"expert": (me_e + 1) % groups},
            device_id_type=MESH,
        )

    def passed(buffer, index, sems, way, p, step):
        send, recv = sems
        return pltpu.make_async_remote_copy(
            src_ref=buffer[0].at[index],
            dst_ref=buffer[1].at[index],
            send_sem=send.at[way, p, step - 1],
            recv_sem=recv.at[way, p, step - 1],
            device_id={"tensor": toward[way]},
            device_id_type=MESH,
        )

    halves = ((R, OUT), (L_, BACK))
    ag_copies, rs_copies, ret_copies, dp_copies, stores = {}, {}, [], [], []

    def gather(p, step):
        for way, part in halves:
            owner = (me_x + (ring - step + 1 if way == R else step - 1)) % ring
            index = (p, owner, part) if step == half else (p, owner)
            copy = passed((ag, ag), index, (ag_send, ag_recv), way, p, step)
            copy.start()
            ag_copies[way, p, step] = copy

    def absorb(p, owner, first=False):
        h = dot(ag[p, owner, OUT], wgu[owner], NN)
        a = dot(ag[p, owner, BACK], wo[owner], NT)
        if first:
            acc_h[p] = h
            acc_a[p] = a
        else:
            acc_h[p] += h
            acc_a[p] += a

    def enter(p):
        if p == 0:
            own.wait()
            many(land, 1, batch - 1, a2a_send.at[0], land_sem.at[0]).wait_recv()
        else:
            many(land, 0, batch, a2a_send.at[0], land_sem.at[p]).wait_recv()
        packed = dot(squeeze[...], land[p * batch : (p + 1) * batch].reshape(block, wide), NN)
        packed = packed.astype(BF16)
        ag[p, me_x, OUT] = packed[:brow]
        ag[p, me_x, BACK] = packed[brow:]
        gather(p, 1)
        if p == 0:
            for copy in weight_copies:
                copy.wait()
        absorb(p, me_x, first=True)

    def forward(p, step):
        for way in (R, L_):
            ag_copies[way, p, step].wait_recv()
        if step < half:
            gather(p, step + 1)
            absorb(p, (me_x + ring - step) % ring)
        absorb(p, (me_x + step) % ring)

    def activate(p):
        pre_gate, pre_up, act_grad = acc_h[p, :, :hid], acc_h[p, :, hid:], acc_a[p]
        sig = jax.nn.sigmoid(pre_gate)
        silu = pre_gate * sig
        act[p] = (silu * pre_up).astype(BF16)
        gug[p, :, :hid] = (act_grad * pre_up * sig * (1.0 + pre_gate * (1.0 - sig))).astype(BF16)
        gug[p, :, hid:] = (act_grad * silu).astype(BF16)

    def contribution(p, part, owner):
        if part == OUT:
            return dot(act[p], wo[owner], NN)
        return dot(gug[p], wgu[owner], NT)

    def push(p, step):
        ahead = half + 1 - step
        for way, part in halves:
            owner = (me_x + (ahead if way == R else ring - ahead)) % ring
            if step == 1:
                rs_send[way, p, 0, part] = contribution(p, part, owner).astype(BF16)
                index = (way, p, 0, part)
            else:
                values = [contribution(p, both, owner) for both in (OUT, BACK)]
                rs_copies[way, p, step - 1].wait_recv()
                for both in (OUT, BACK):
                    if step > 2 or both == part:
                        values[both] = values[both] + rs_recv[way, p, step - 2, both].astype(F32)
                    rs_send[way, p, step - 1, both] = values[both].astype(BF16)
                index = (way, p, step - 1)
            copy = passed((rs_send, rs_recv), index, (rs_ssem, rs_rsem), way, p, step)
            copy.start()
            rs_copies[way, p, step] = copy

    def leave(p):
        values = [contribution(p, both, me_x) for both in (OUT, BACK)]
        for way, part in halves:
            rs_copies[way, p, half].wait_recv()
            for both in (OUT, BACK):
                if half > 1 or both == part:
                    values[both] = values[both] + rs_recv[way, p, half - 1, both].astype(F32)
        for both in (OUT, BACK):
            fin[p, pl.ds(both * brow, brow), :] = values[both].astype(BF16)
        spread = dot(stretch[...], fin[p], NN).astype(BF16)
        ret[p * batch : (p + 1) * batch] = spread.reshape(batch, 2 * PAD, wide)

        @pl.loop(1 if p == 0 else 0, batch)
        def _(q):
            there = other(p, q, -1)
            pltpu.make_async_remote_copy(
                src_ref=ret.at[p * batch + q],
                dst_ref=home.at[me_e],
                send_sem=a2a_send.at[1],
                recv_sem=home_sem.at[0],
                device_id={"expert": there},
                device_id_type=MESH,
            ).start()

        if p == 0:
            ret_copies.append(pltpu.make_async_copy(ret.at[0], home.at[me_e], own_sem.at[1]))
            ret_copies[0].start()

    def grads_of(owner):
        lat = ag[:, owner, OUT].reshape(rows, wide)
        cots = ag[:, owner, BACK].reshape(rows, wide)
        return dot(lat, gug[...].reshape(rows, 2 * hid), TN), dot(act_t[...], cots, NN)

    def for_peer(i):
        if i == 0:
            act_t[...] = act[...].reshape(rows, hid).T
        gu, o = grads_of(peer_d * half + i)
        dp_gu_send[i] = gu.astype(BF16)
        dp_o_send[i] = o.astype(BF16)
        for j, (src, dst) in enumerate(((dp_gu_send, dp_gu_recv), (dp_o_send, dp_o_recv))):
            copy = pltpu.make_async_remote_copy(
                src_ref=src.at[i],
                dst_ref=dst.at[i],
                send_sem=dp_ssem.at[j, i],
                recv_sem=dp_rsem.at[j, i],
                device_id={"dp": peer_d},
                device_id_type=MESH,
            )
            copy.start()
            dp_copies.append(copy)

    def for_self(i):
        gu, o = grads_of(me_d * half + i)
        for copy in dp_copies[2 * i : 2 * i + 2]:
            copy.wait_recv()
        stage_gu[i] = (gu + dp_gu_recv[i].astype(F32)).astype(BF16)
        stage_o[i] = (o + dp_o_recv[i].astype(F32)).astype(BF16)
        for j, (src, dst) in enumerate(
            (
                (stage_gu.at[i, :, pl.ds(0, hid)], grad_gate.at[0, pl.ds(i * wide, wide), :]),
                (stage_gu.at[i, :, pl.ds(hid, hid)], grad_up.at[0, pl.ds(i * wide, wide), :]),
                (stage_o.at[i], grad_out.at[0, :, pl.ds(i * wide, wide)]),
            )
        ):
            copy = pltpu.make_async_copy(src, dst, store_sem.at[j, i])
            copy.start()
            stores.append(copy)

    tasks = [functools.partial(for_peer, i) for i in range(half)]
    tasks += [functools.partial(for_self, i) for i in range(half)]

    for tick in range(2 * half + batches):
        if tick < batches:
            enter(tick)
        for p in range(batches):
            at = tick - p
            if 1 <= at <= half:
                forward(p, at)
                if at == half:
                    activate(p)
                    push(p, 1)
            elif half < at < 2 * half:
                push(p, at - half + 1)
            elif at == 2 * half:
                leave(p)
            if tick > half + batches - 1 and tasks:
                tasks.pop(0)()
    for task in tasks:
        task()

    for copy in (*ag_copies.values(), *rs_copies.values(), *dp_copies):
        copy.wait_send()
    for copy in stores:
        copy.wait()
    many(disp, 0, groups - 1, a2a_send.at[0], land_sem.at[0]).wait_send()

    for copy in ret_copies:
        copy.wait()
    homeward = many(home, 0, groups - 1, a2a_send.at[1], home_sem.at[0])
    homeward.wait_recv()
    back = home[...].reshape(groups * 2 * PAD, wide)
    latent_out[...] = dot(comb[0], back, NN).astype(BF16)
    latent_grad[...] = dot(comb[1], back, NN).astype(BF16)
    homeward.wait_send()


def hand_on(*refs):
    count = (len(refs) - 1) // 2
    copies = [
        pltpu.make_async_copy(refs[i], refs[count + i], refs[-1].at[i]) for i in range(count)
    ]
    for copy in copies:
        copy.start()
    for copy in copies:
        copy.wait()


def per_device(tokens, w_latent, w_gate, w_up, w_out, expert_ids, gates, cotangent):
    groups, ring = lax.axis_size("expert"), lax.axis_size("tensor")
    half = ring // 2
    tok, width = tokens.shape
    wide = cotangent.shape[1]
    hid = w_gate.shape[2]
    rows = groups * CAP
    span = 1
    while (2 * span) ** 2 <= groups:
        span = 2 * span
    batch, batches = 2 * span, groups // (2 * span)
    brow, block = batch * CAP, batch * 2 * PAD
    lat_steps = 8
    depth = width // lat_steps
    dma = pltpu.SemaphoreType.DMA
    vmem = pl.BlockSpec(memory_space=pltpu.VMEM)
    hbm = pl.BlockSpec(memory_space=pl.ANY)
    flops = 2 * tok * width * wide + 18 * rows * ring * wide * hid
    outs = pl.pallas_call(
        functools.partial(kernel, (groups, span, ring, lat_steps)),
        out_shape=(
            jax.ShapeDtypeStruct((tok, wide), BF16),
            jax.ShapeDtypeStruct((tok, wide), BF16),
            jax.ShapeDtypeStruct((1, half * wide, hid), BF16),
            jax.ShapeDtypeStruct((1, half * wide, hid), BF16),
            jax.ShapeDtypeStruct((1, hid, half * wide), BF16),
        ),
        in_specs=[hbm] * 5 + [vmem] * 3,
        out_specs=(vmem, vmem, hbm, hbm, hbm),
        scratch_shapes=[
            pltpu.VMEM((lat_steps, tok, depth), BF16),
            pltpu.VMEM((lat_steps, depth, wide), BF16),
            pltpu.VMEM((ring, wide, 2 * hid), BF16),
            pltpu.VMEM((ring, hid, wide), BF16),
            pltpu.VMEM((2, tok, groups * 2 * PAD), BF16),
            pltpu.VMEM((groups, 2 * PAD, wide), BF16),
            pltpu.VMEM((groups, 2 * PAD, wide), BF16),
            pltpu.VMEM((batches, ring, 2, brow, wide), BF16),
            pltpu.VMEM((batches, brow, 2 * hid), F32),
            pltpu.VMEM((batches, brow, hid), F32),
            pltpu.VMEM((batches, brow, hid), BF16),
            pltpu.VMEM((hid, rows), BF16),
            pltpu.VMEM((batches, brow, 2 * hid), BF16),
            pltpu.VMEM((2, batches, half, 2, brow, wide), BF16),
            pltpu.VMEM((2, batches, half, 2, brow, wide), BF16),
            pltpu.VMEM((batches, 2 * brow, wide), BF16),
            pltpu.VMEM((groups, 2 * PAD, wide), BF16),
            pltpu.VMEM((groups, 2 * PAD, wide), BF16),
            pltpu.VMEM((2 * brow, block), BF16),
            pltpu.VMEM((block, 2 * brow), BF16),
            pltpu.VMEM((half, wide, 2 * hid), BF16),
            pltpu.VMEM((half, wide, 2 * hid), BF16),
            pltpu.VMEM((half, hid, wide), BF16),
            pltpu.VMEM((half, hid, wide), BF16),
            pltpu.VMEM((half, wide, 2 * hid), BF16),
            pltpu.VMEM((half, hid, wide), BF16),
            dma((3, ring)),
            dma((2, lat_steps)),
            dma((2,)),
            dma((2,)),
            dma((batches,)),
            dma((1,)),
            dma((2, batches, half)),
            dma((2, batches, half)),
            dma((2, batches, half)),
            dma((2, batches, half)),
            dma((2, half)),
            dma((2, half)),
            dma((3, half)),
        ],
        compiler_params=pltpu.CompilerParams(
            collective_id=0, has_side_effects=True, vmem_limit_bytes=56 * 1024 * 1024
        ),
        cost_estimate=pl.CostEstimate(
            flops=flops, bytes_accessed=10 * 1024 * 1024, transcendentals=rows * hid
        ),
    )(tokens, w_latent, w_gate, w_up, w_out, expert_ids.T, gates.T, cotangent)
    return pl.pallas_call(
        hand_on,
        out_shape=tuple(jax.ShapeDtypeStruct(out.shape, out.dtype) for out in outs),
        in_specs=[hbm] * len(outs),
        out_specs=(hbm,) * len(outs),
        scratch_shapes=[dma((len(outs),))],
    )(*outs)


def solution(mesh):
    in_specs = (
        P(("dp", "expert"), None),
        P(None, "tensor"),
        P("expert", None, "tensor"),
        P("expert", None, "tensor"),
        P("expert", "tensor", None),
        P(("dp", "expert"), None),
        P(("dp", "expert"), None),
        P(("dp", "expert"), "tensor"),
    )
    out_specs = (
        P(("dp", "expert"), "tensor"),
        P(("dp", "expert"), "tensor"),
        P("expert", "dp", "tensor"),
        P("expert", "dp", "tensor"),
        P("expert", "tensor", "dp"),
    )
    return jax.shard_map(
        per_device, mesh=mesh, in_specs=in_specs, out_specs=out_specs, check_vma=False
    )
```

time: 129 us -> 162 us (1.26)
  the two profiles are of different devices: /device:TPU:4 before, /device:TPU:2 now
where the time goes in v2:
time: 162 us
  Pallas kernels  161 us (99%)
    pallas_call x1, Pallas kernels, per_device(): pl.pallas_call(functools.partial(kernel, (groups, span, ring, lat_steps))...  111 us
    pallas_call x1, Pallas kernels, per_device(): pl.pallas_call(hand_on, out_shape=tuple((jax.ShapeDtypeStruct(out.shape,...  49.8 us

profile of v2, /device:TPU:2, one launch (start us, length us, event | category | flops | bytes accessed | tf_op | source)
XLA Modules:
  0.0 161.8 jit_solution(13690714122927076554)
XLA Ops:
  0.6 111.3 %shard_map.119 = (bf16[32,256]{1,0:T(8,128)(2,1)}, bf16[32,256]{1,0:T(8,128)(2,1)}, bf16[1,1024,256]{2,1,0:T(8,128)(2,1)}, bf16[1,1024,256]{2,1,0:T(8,128)(2,1)}, bf16[1,256,1024]{2,1,0:T(8,128)(2,1)}) custom-call(bf16[32,8192]{1,0:T(8,128)(2,1)} %tokens.1, bf16[8192,256]{1,0:T(8,128)(2,1)} %w_latent.1, bf16[1,2048,256]{2,1,0:T(8,128)(2,1)} %w_gate.1, ...), custom_call_target="tpu_custom_call" | custom-call | flops 3758096384 | bytes 10485760 | tf_op jit(solution)/shard_map/pallas_call | solution.py:460
  112.0 49.8 %shard_map.120 = (bf16[32,256]{1,0:T(8,128)(2,1)}, bf16[32,256]{1,0:T(8,128)(2,1)}, bf16[1,1024,256]{2,1,0:T(8,128)(2,1)}, bf16[1,1024,256]{2,1,0:T(8,128)(2,1)}, bf16[1,256,1024]{2,1,0:T(8,128)(2,1)}) custom-call(bf16[32,256]{1,0:T(8,128)(2,1)} %get-tuple-element.10.refs_0_, bf16[32,256]{1,0:T(8,128)(2,1)} %get-tuple-element.11.refs_1_, ...), custom_call_target="tpu_custom_call" | custom-call | tf_op jit(solution)/shard_map/pallas_call | solution.py:519

commit v3 on v2

--- a/solution.py
+++ b/solution.py
@@ -396,7 +396,7 @@
     for tick in range(2 * half + batches):
         if tick < batches:
             enter(tick)
-        for p in range(batches):
+        for p in reversed(range(batches)):
             at = tick - p
             if 1 <= at <= half:
                 forward(p, at)
@@ -428,14 +428,17 @@
     homeward.wait_send()
 
 
-def hand_on(*refs):
-    count = (len(refs) - 1) // 2
-    copies = [
-        pltpu.make_async_copy(refs[i], refs[count + i], refs[-1].at[i]) for i in range(count)
-    ]
-    for copy in copies:
+def hand_on(count, *refs):
+    given, results, held = refs[:count], refs[count : 2 * count], refs[2 * count : 3 * count]
+    sems = refs[-1]
+    loads = [pltpu.make_async_copy(given[i], held[i], sems.at[0, i]) for i in range(count)]
+    stores = [pltpu.make_async_copy(held[i], results[i], sems.at[1, i]) for i in range(count)]
+    for copy in loads:
         copy.start()
-    for copy in copies:
+    for load, store in zip(loads, stores):
+        load.wait()
+        store.start()
+    for copy in stores:
         copy.wait()
 
 
@@ -517,11 +520,12 @@
         ),
     )(tokens, w_latent, w_gate, w_up, w_out, expert_ids.T, gates.T, cotangent)
     return pl.pallas_call(
-        hand_on,
+        functools.partial(hand_on, len(outs)),
         out_shape=tuple(jax.ShapeDtypeStruct(out.shape, out.dtype) for out in outs),
         in_specs=[hbm] * len(outs),
         out_specs=(hbm,) * len(outs),
-        scratch_shapes=[dma((len(outs),))],
+        scratch_shapes=[pltpu.VMEM(out.shape, out.dtype) for out in outs] + [dma((2, len(outs)))],
+        compiler_params=pltpu.CompilerParams(vmem_limit_bytes=60 * 1024 * 1024),
     )(*outs)
 
 

time: 162 us -> 110 us (0.68)
  the two profiles are of different devices: /device:TPU:2 before, /device:TPU:4 now
where the time goes in v3:
time: 110 us
  Pallas kernels  109 us (99%)
    pallas_call x1, Pallas kernels, per_device(): pl.pallas_call(functools.partial(kernel, (groups, span, ring, lat_steps))...  107 us
    pallas_call x1, Pallas kernels, per_device(): pl.pallas_call(functools.partial(hand_on, len(outs)), out_shape=tuple((ja...  2.3 us

profile of v3, /device:TPU:4, one launch (start us, length us, event | category | flops | bytes accessed | tf_op | source)
XLA Modules:
  0.0 110.0 jit_solution(15525448598241889581)
XLA Ops:
  0.6 107.0 %shard_map.119 = (bf16[32,256]{1,0:T(8,128)(2,1)}, bf16[32,256]{1,0:T(8,128)(2,1)}, bf16[1,1024,256]{2,1,0:T(8,128)(2,1)}, bf16[1,1024,256]{2,1,0:T(8,128)(2,1)}, bf16[1,256,1024]{2,1,0:T(8,128)(2,1)}) custom-call(bf16[32,8192]{1,0:T(8,128)(2,1)} %tokens.1, bf16[8192,256]{1,0:T(8,128)(2,1)} %w_latent.1, bf16[1,2048,256]{2,1,0:T(8,128)(2,1)} %w_gate.1, ...), custom_call_target="tpu_custom_call" | custom-call | flops 3758096384 | bytes 10485760 | tf_op jit(solution)/shard_map/pallas_call | solution.py:463
  107.7 2.3 %shard_map.120 = (bf16[32,256]{1,0:T(8,128)(2,1)}, bf16[32,256]{1,0:T(8,128)(2,1)}, bf16[1,1024,256]{2,1,0:T(8,128)(2,1)}, bf16[1,1024,256]{2,1,0:T(8,128)(2,1)}, bf16[1,256,1024]{2,1,0:T(8,128)(2,1)}) custom-call(bf16[32,256]{1,0:T(8,128)(2,1)} %get-tuple-element.10.refs_0_, bf16[32,256]{1,0:T(8,128)(2,1)} %get-tuple-element.11.refs_1_, ...), custom_call_target="tpu_custom_call" | custom-call | tf_op jit(solution)/shard_map/pallas_call | solution.py:522

commit v4 on v3

--- a/solution.py
+++ b/solution.py
@@ -133,18 +133,6 @@
     peer_d = 1 - me_d
     toward = ((me_x + 1) % ring, (me_x + ring - 1) % ring)
 
-    barrier = pltpu.get_barrier_semaphore()
-
-    @pl.loop(1, groups)
-    def _(i):
-        pl.semaphore_signal(
-            barrier, 1, device_id={"expert": (me_e + i) % groups}, device_id_type=MESH
-        )
-
-    for there in toward:
-        pl.semaphore_signal(barrier, 1, device_id={"tensor": there}, device_id_type=MESH)
-    pl.semaphore_signal(barrier, 1, device_id={"dp": peer_d}, device_id_type=MESH)
-
     depth = wl_v.shape[1]
     lat_copies = []
     for i in range(lat_steps):
@@ -161,18 +149,27 @@
     for pair in lat_copies:
         for copy in pair:
             copy.start()
-    weight_copies = []
+    barrier = pltpu.get_barrier_semaphore()
+
+    @pl.loop(1, groups)
+    def _(i):
+        pl.semaphore_signal(
+            barrier, 1, device_id={"expert": (me_e + i) % groups}, device_id_type=MESH
+        )
+
+    for there in toward:
+        pl.semaphore_signal(barrier, 1, device_id={"tensor": there}, device_id_type=MESH)
+    pl.semaphore_signal(barrier, 1, device_id={"dp": peer_d}, device_id_type=MESH)
+
+    weight_copies = [
+        pltpu.make_async_copy(w_gate, wgu.at[:, :, pl.ds(0, hid)], load_sem.at[0]),
+        pltpu.make_async_copy(w_up, wgu.at[:, :, pl.ds(hid, hid)], load_sem.at[1]),
+    ]
     for i in range(ring):
-        for which, copy_of in enumerate(
-            (
-                (w_gate.at[0, pl.ds(i * wide, wide), :], wgu.at[i, :, pl.ds(0, hid)]),
-                (w_up.at[0, pl.ds(i * wide, wide), :], wgu.at[i, :, pl.ds(hid, hid)]),
-                (w_out.at[0, :, pl.ds(i * wide, wide)], wo.at[i]),
-            )
-        ):
-            copy = pltpu.make_async_copy(*copy_of, load_sem.at[which, i])
-            copy.start()
-            weight_copies.append(copy)
+        part = w_out.at[0, :, pl.ds(i * wide, wide)]
+        weight_copies.append(pltpu.make_async_copy(part, wo.at[i], load_sem.at[2 + i]))
+    for copy in weight_copies:
+        copy.start()
 
     here, scaled, forward = slot_maps(ids[...], gates[...], groups)
     comb[0] = jnp.where(forward, scaled, 0.0).astype(BF16)
@@ -195,33 +192,43 @@
 
     me_line, me_place = me_e // span, me_e % span
 
-    def other(p, q, sign):
-        odd, line_odd = (q // 2) % 2, q % 2
-        by = q // 4
-        d_place = by + odd * (span - 1 - 2 * by)
-        d_line = p + line_odd * (lines - 1 - 2 * p)
-        if sign < 0:
-            d_place, d_line = span - d_place, lines - d_line
-        return ((me_line + d_line) % lines) * span + (me_place + d_place) % span
-
-    def dispatch_copy(p, q):
-        there = other(p, q, 1)
-        return pltpu.make_async_remote_copy(
-            src_ref=disp.at[there],
-            dst_ref=land.at[p * batch + q],
-            send_sem=a2a_send.at[0],
-            recv_sem=land_sem.at[p],
-            device_id={"expert": there},
-            device_id_type=MESH,
-        )
-
+    def to_batch(p, sign, send):
+        lines_there = [
+            (me_line + (by if sign > 0 else lines - by)) % lines for by in (p, lines - 1 - p)
+        ]
+
+        def four(by, skip):
+            for odd in (0, 1):
+                place = by + odd * (span - 1 - 2 * by)
+                place_there = (me_place + (place if sign > 0 else span - place)) % span
+                for line_odd in (0, 1):
+                    if not (skip and odd == 0 and line_odd == 0):
+                        q = 4 * by + 2 * odd + line_odd
+                        send(p * batch + q, lines_there[line_odd] * span + place_there)
+
+        if p == 0:
+            four(0, True)
+        if p > 0 or span > 2:
+            pl.loop(1 if p == 0 else 0, span // 2)(lambda by: four(by, False))
+
+    def dispatch(p):
+        def send(index, there):
+            pltpu.make_async_remote_copy(
+                src_ref=disp.at[there],
+                dst_ref=land.at[index],
+                send_sem=a2a_send.at[0],
+                recv_sem=land_sem.at[p],
+                device_id={"expert": there},
+                device_id_type=MESH,
+            ).start()
+
+        to_batch(p, 1, send)
+
+    order = [*range(1, batches), 0]
     own = pltpu.make_async_copy(disp.at[me_e], land.at[0], own_sem.at[0])
     own.start()
-    for p in range(batches):
-
-        @pl.loop(1 if p == 0 else 0, batch)
-        def _(q, p=p):
-            dispatch_copy(p, q).start()
+    for p in order[:2]:
+        dispatch(p)
 
     def many(buffer, first, count, send_sem, recv_sem):
         part = buffer.at[pl.ds(first, count)]
@@ -277,7 +284,9 @@
         ag[p, me_x, OUT] = packed[:brow]
         ag[p, me_x, BACK] = packed[brow:]
         gather(p, 1)
-        if p == 0:
+        if p in order[:-2]:
+            dispatch(order[order.index(p) + 2])
+        if p == order[0]:
             for copy in weight_copies:
                 copy.wait()
         absorb(p, me_x, first=True)
@@ -334,17 +343,17 @@
         spread = dot(stretch[...], fin[p], NN).astype(BF16)
         ret[p * batch : (p + 1) * batch] = spread.reshape(batch, 2 * PAD, wide)
 
-        @pl.loop(1 if p == 0 else 0, batch)
-        def _(q):
-            there = other(p, q, -1)
+        def send(index, there):
             pltpu.make_async_remote_copy(
-                src_ref=ret.at[p * batch + q],
+                src_ref=ret.at[index],
                 dst_ref=home.at[me_e],
                 send_sem=a2a_send.at[1],
                 recv_sem=home_sem.at[0],
                 device_id={"expert": there},
                 device_id_type=MESH,
             ).start()
+
+        to_batch(p, -1, send)
 
         if p == 0:
             ret_copies.append(pltpu.make_async_copy(ret.at[0], home.at[me_e], own_sem.at[1]))
@@ -395,9 +404,9 @@
 
     for tick in range(2 * half + batches):
         if tick < batches:
-            enter(tick)
-        for p in reversed(range(batches)):
-            at = tick - p
+            enter(order[tick])
+        for place, p in reversed(list(enumerate(order))):
+            at = tick - place
             if 1 <= at <= half:
                 forward(p, at)
                 if at == half:
@@ -498,7 +507,7 @@
             pltpu.VMEM((half, hid, wide), BF16),
             pltpu.VMEM((half, wide, 2 * hid), BF16),
             pltpu.VMEM((half, hid, wide), BF16),
-            dma((3, ring)),
+            dma((2 + ring,)),
             dma((2, lat_steps)),
             dma((2,)),
             dma((2,)),
@@ -518,7 +527,16 @@
         cost_estimate=pl.CostEstimate(
             flops=flops, bytes_accessed=10 * 1024 * 1024, transcendentals=rows * hid
         ),
-    )(tokens, w_latent, w_gate, w_up, w_out, expert_ids.T, gates.T, cotangent)
+    )(
+        tokens,
+        w_latent,
+        w_gate.reshape(ring, wide, hid),
+        w_up.reshape(ring, wide, hid),
+        w_out,
+        expert_ids.T,
+        gates.T,
+        cotangent,
+    )
     return pl.pallas_call(
         functools.partial(hand_on, len(outs)),
         out_shape=tuple(jax.ShapeDtypeStruct(out.shape, out.dtype) for out in outs),

time: 110 us -> 109 us (level)
  the two profiles are of different devices: /device:TPU:4 before, /device:TPU:16 now
where the time goes in v4:
time: 109 us
  Pallas kernels  108 us (99%)
    pallas_call x1, Pallas kernels, per_device(): pl.pallas_call(functools.partial(kernel, (groups, span, ring, lat_steps))...  106 us
    pallas_call x1, Pallas kernels, per_device(): pl.pallas_call(functools.partial(hand_on, len(outs)), out_shape=tuple((ja...  2.3 us

profile of v4, /device:TPU:16, one launch (start us, length us, event | category | flops | bytes accessed | tf_op | source)
XLA Modules:
  0.0 108.8 jit_solution(1270080678515751934)
XLA Ops:
  0.6 105.9 %shard_map.119 = (bf16[32,256]{1,0:T(8,128)(2,1)}, bf16[32,256]{1,0:T(8,128)(2,1)}, bf16[1,1024,256]{2,1,0:T(8,128)(2,1)}, bf16[1,1024,256]{2,1,0:T(8,128)(2,1)}, bf16[1,256,1024]{2,1,0:T(8,128)(2,1)}) custom-call(bf16[32,8192]{1,0:T(8,128)(2,1)} %tokens.1, bf16[8192,256]{1,0:T(8,128)(2,1)} %w_latent.1, bf16[8,256,256]{2,1,0:T(8,128)(2,1)} %bitcast.4, ...), custom_call_target="tpu_custom_call" | custom-call | flops 3758096384 | bytes 10485760 | tf_op jit(solution)/shard_map/pallas_call | solution.py:472
  106.5 2.3 %shard_map.120 = (bf16[32,256]{1,0:T(8,128)(2,1)}, bf16[32,256]{1,0:T(8,128)(2,1)}, bf16[1,1024,256]{2,1,0:T(8,128)(2,1)}, bf16[1,1024,256]{2,1,0:T(8,128)(2,1)}, bf16[1,256,1024]{2,1,0:T(8,128)(2,1)}) custom-call(bf16[32,256]{1,0:T(8,128)(2,1)} %get-tuple-element.10.refs_0_, bf16[32,256]{1,0:T(8,128)(2,1)} %get-tuple-element.11.refs_1_, ...), custom_call_target="tpu_custom_call" | custom-call | tf_op jit(solution)/shard_map/pallas_call | solution.py:540

commit v5 on v4

--- a/solution.py
+++ b/solution.py
@@ -25,7 +25,7 @@
 TN = ((0,), (0,))
 
 
-def slot_maps(ids, gates, groups):
+def slot_maps(ids, gates, groups, near):
     top, tok = ids.shape
     expert = lax.broadcasted_iota(jnp.int32, (groups, tok), 0)
     member = jnp.zeros((groups, tok), F32)
@@ -38,21 +38,25 @@
         jnp.int32, (tok, tok), 1
     )
     place = dot(member.astype(BF16), jnp.where(earlier, 1.0, 0.0).astype(BF16), NN)
-    cols = groups * 2 * PAD
-    widen = jnp.where(
-        lax.shift_right_logical(lax.broadcasted_iota(jnp.int32, (groups, cols), 1), 4)
-        == lax.broadcasted_iota(jnp.int32, (groups, cols), 0),
-        1.0,
-        0.0,
-    ).astype(BF16)
-    col = lax.broadcasted_iota(jnp.int32, (tok, cols), 1)
-    slot = lax.bitwise_and(col, PAD - 1).astype(F32)
-    part = lax.bitwise_and(col, PAD)
-    here = jnp.where(
-        dot(place.astype(BF16), widen, TN) == slot, dot(member.astype(BF16), widen, TN), 0.0
+
+    def spread(cols, owner_of):
+        widen = jnp.where(
+            owner_of(lax.broadcasted_iota(jnp.int32, (groups, cols), 1))
+            == lax.broadcasted_iota(jnp.int32, (groups, cols), 0),
+            1.0,
+            0.0,
+        ).astype(BF16)
+        col = lax.broadcasted_iota(jnp.int32, (tok, cols), 1)
+        slot = lax.bitwise_and(col, PAD - 1).astype(F32)
+        here = jnp.where(
+            dot(place.astype(BF16), widen, TN) == slot, dot(member.astype(BF16), widen, TN), 0.0
+        )
+        return here, here * dot(weight.astype(BF16), widen, TN), lax.bitwise_and(col, PAD) == 0
+
+    return (
+        spread(groups * 2 * PAD, lambda col: lax.shift_right_logical(col, 4)),
+        spread(near[0] * 2 * PAD, near[1]),
     )
-    scaled = here * dot(weight.astype(BF16), widen, TN)
-    return here, scaled, part == 0
 
 
 def picks(shape, row_dim, brow):
@@ -99,6 +103,10 @@
     home,
     squeeze,
     stretch,
+    near_map,
+    cot_all,
+    disp_wide,
+    land_wide,
     dp_gu_send,
     dp_gu_recv,
     dp_o_send,
@@ -111,6 +119,9 @@
     a2a_send,
     land_sem,
     home_sem,
+    wide_sem,
+    cot_send,
+    cot_recv,
     ag_send,
     ag_recv,
     rs_ssem,
@@ -157,8 +168,10 @@
             barrier, 1, device_id={"expert": (me_e + i) % groups}, device_id_type=MESH
         )
 
-    for there in toward:
-        pl.semaphore_signal(barrier, 1, device_id={"tensor": there}, device_id_type=MESH)
+    for i in range(1, ring):
+        pl.semaphore_signal(
+            barrier, 1, device_id={"tensor": (me_x + i) % ring}, device_id_type=MESH
+        )
     pl.semaphore_signal(barrier, 1, device_id={"dp": peer_d}, device_id_type=MESH)
 
     weight_copies = [
@@ -171,7 +184,23 @@
     for copy in weight_copies:
         copy.start()
 
-    here, scaled, forward = slot_maps(ids[...], gates[...], groups)
+    me_line, me_place = me_e // span, me_e % span
+
+    def near_expert(col):
+        q = lax.shift_right_logical(col, 4)
+        by = lax.shift_right_logical(q, 2)
+        odd = lax.bitwise_and(lax.shift_right_logical(q, 1), 1)
+        place = by + odd * (span - 1 - 2 * by)
+        line = lax.bitwise_and(q, 1) * (lines - 1)
+        return lax.bitwise_and(me_line + line, lines - 1) * span + lax.bitwise_and(
+            me_place + place, span - 1
+        )
+
+    maps = slot_maps(ids[...], gates[...], groups, (batch, near_expert))
+    (here, scaled, forward), (_, near_scaled, near_first) = maps
+    near_map[0] = jnp.where(near_first, near_scaled, 0.0).astype(BF16)
+    near_map[1] = jnp.where(near_first, 0.0, near_scaled).astype(BF16)
+    cot_all[me_x] = cot[...]
     comb[0] = jnp.where(forward, scaled, 0.0).astype(BF16)
     comb[1] = jnp.where(forward, 0.0, here).astype(BF16)
     to_rows = jnp.where(forward, here, 0.0).astype(BF16)
@@ -188,9 +217,19 @@
     )
     squeeze[...] = picks((2 * brow, block), 0, brow)
     stretch[...] = picks((block, 2 * brow), 1, brow)
-    pl.semaphore_wait(barrier, groups + 2)
-
-    me_line, me_place = me_e // span, me_e % span
+    pl.semaphore_wait(barrier, groups + ring - 1)
+
+    cot_copies = []
+    for i in range(1, ring):
+        copy = pltpu.make_async_remote_copy(
+            src_ref=cot,
+            dst_ref=cot_all.at[me_x],
+            send_sem=cot_send.at[i - 1],
+            recv_sem=cot_recv.at[i - 1],
+            device_id={"tensor": (me_x + i) % ring},
+            device_id_type=MESH,
+        )
+        cot_copies.append(copy)
 
     def to_batch(p, sign, send):
         lines_there = [
@@ -229,6 +268,41 @@
     own.start()
     for p in order[:2]:
         dispatch(p)
+    for copy in cot_copies:
+        copy.start()
+
+    def dispatch_wide():
+        for copy in cot_copies:
+            copy.wait_recv()
+        for s in range(half):
+            part = dot(near_map[0], cot_all[s], TN) + dot(near_map[1], cot_all[half + s], TN)
+            part = part.astype(BF16).reshape(batch, 2 * PAD, wide)
+            disp_wide[:, :, s * wide : (s + 1) * wide] = part
+
+        def send(index, there):
+            pltpu.make_async_remote_copy(
+                src_ref=disp_wide.at[index],
+                dst_ref=land_wide.at[index],
+                send_sem=wide_sem.at[0],
+                recv_sem=wide_sem.at[1],
+                device_id={"expert": there},
+                device_id_type=MESH,
+            ).start()
+
+        to_batch(0, 1, send)
+        pltpu.make_async_copy(disp_wide.at[0], land_wide.at[0], own_sem.at[2]).start()
+
+    def enter_wide():
+        pltpu.make_async_copy(disp_wide.at[0], land_wide.at[0], own_sem.at[2]).wait()
+        many(land_wide, 1, batch - 1, wide_sem.at[0], wide_sem.at[1]).wait_recv()
+        total = jnp.zeros((brow, hid), F32)
+        for s in range(half):
+            part = land_wide[:, :, s * wide : (s + 1) * wide].reshape(block, wide)
+            packed = dot(squeeze[...], part, NN).astype(BF16)
+            ag[0, s, BACK] = packed[:brow]
+            ag[0, half + s, BACK] = packed[brow:]
+            total = total + dot(packed[:brow], wo[s], NT) + dot(packed[brow:], wo[half + s], NT)
+        acc_a[0] = total
 
     def many(buffer, first, count, send_sem, recv_sem):
         part = buffer.at[pl.ds(first, count)]
@@ -259,19 +333,26 @@
         for way, part in halves:
             owner = (me_x + (ring - step + 1 if way == R else step - 1)) % ring
             index = (p, owner, part) if step == half else (p, owner)
+            if p == 0:
+                if step == half and part == BACK:
+                    continue
+                index = (p, owner, OUT)
             copy = passed((ag, ag), index, (ag_send, ag_recv), way, p, step)
             copy.start()
             ag_copies[way, p, step] = copy
 
     def absorb(p, owner, first=False):
         h = dot(ag[p, owner, OUT], wgu[owner], NN)
-        a = dot(ag[p, owner, BACK], wo[owner], NT)
         if first:
             acc_h[p] = h
-            acc_a[p] = a
         else:
             acc_h[p] += h
-            acc_a[p] += a
+        if p > 0:
+            a = dot(ag[p, owner, BACK], wo[owner], NT)
+            if first:
+                acc_a[p] = a
+            else:
+                acc_a[p] += a
 
     def enter(p):
         if p == 0:
@@ -282,7 +363,8 @@
         packed = dot(squeeze[...], land[p * batch : (p + 1) * batch].reshape(block, wide), NN)
         packed = packed.astype(BF16)
         ag[p, me_x, OUT] = packed[:brow]
-        ag[p, me_x, BACK] = packed[brow:]
+        if p > 0:
+            ag[p, me_x, BACK] = packed[brow:]
         gather(p, 1)
         if p in order[:-2]:
             dispatch(order[order.index(p) + 2])
@@ -293,7 +375,8 @@
 
     def forward(p, step):
         for way in (R, L_):
-            ag_copies[way, p, step].wait_recv()
+            if (way, p, step) in ag_copies:
+                ag_copies[way, p, step].wait_recv()
         if step < half:
             gather(p, step + 1)
             absorb(p, (me_x + ring - step) % ring)
@@ -410,6 +493,8 @@
             if 1 <= at <= half:
                 forward(p, at)
                 if at == half:
+                    if p == 0:
+                        enter_wide()
                     activate(p)
                     push(p, 1)
             elif half < at < 2 * half:
@@ -418,10 +503,13 @@
                 leave(p)
             if tick > half + batches - 1 and tasks:
                 tasks.pop(0)()
+        if tick == 1:
+            dispatch_wide()
     for task in tasks:
         task()
 
-    for copy in (*ag_copies.values(), *rs_copies.values(), *dp_copies):
+    many(disp_wide, 1, batch - 1, wide_sem.at[0], wide_sem.at[1]).wait_send()
+    for copy in (*cot_copies, *ag_copies.values(), *rs_copies.values(), *dp_copies):
         copy.wait_send()
     for copy in stores:
         copy.wait()
@@ -501,6 +589,10 @@
             pltpu.VMEM((groups, 2 * PAD, wide), BF16),
             pltpu.VMEM((2 * brow, block), BF16),
             pltpu.VMEM((block, 2 * brow), BF16),
+            pltpu.VMEM((2, tok, block), BF16),
+            pltpu.VMEM((ring, tok, wide), BF16),
+            pltpu.VMEM((batch, 2 * PAD, half * wide), BF16),
+            pltpu.VMEM((batch, 2 * PAD, half * wide), BF16),
             pltpu.VMEM((half, wide, 2 * hid), BF16),
             pltpu.VMEM((half, wide, 2 * hid), BF16),
             pltpu.VMEM((half, hid, wide), BF16),
@@ -509,10 +601,13 @@
             pltpu.VMEM((half, hid, wide), BF16),
             dma((2 + ring,)),
             dma((2, lat_steps)),
-            dma((2,)),
+            dma((3,)),
             dma((2,)),
             dma((batches,)),
             dma((1,)),
+            dma((2,)),
+            dma((ring - 1,)),
+            dma((ring - 1,)),
             dma((2, batches, half)),
             dma((2, batches, half)),
             dma((2, batches, half)),

time: 109 us -> 106 us (0.972)
  the two profiles are of different devices: /device:TPU:16 before, /device:TPU:20 now
where the time goes in v5:
time: 106 us
  Pallas kernels  105 us (99%)
    pallas_call x1, Pallas kernels, per_device(): pl.pallas_call(functools.partial(kernel, (groups, span, ring, lat_steps))...  103 us
    pallas_call x1, Pallas kernels, per_device(): pl.pallas_call(functools.partial(hand_on, len(outs)), out_shape=tuple((ja...  2.3 us

profile of v5, /device:TPU:20, one launch (start us, length us, event | category | flops | bytes accessed | tf_op | source)
XLA Modules:
  0.0 106.1 jit_solution(14582152501359146597)
XLA Ops:
  0.6 103.2 %shard_map.119 = (bf16[32,256]{1,0:T(8,128)(2,1)}, bf16[32,256]{1,0:T(8,128)(2,1)}, bf16[1,1024,256]{2,1,0:T(8,128)(2,1)}, bf16[1,1024,256]{2,1,0:T(8,128)(2,1)}, bf16[1,256,1024]{2,1,0:T(8,128)(2,1)}) custom-call(bf16[32,8192]{1,0:T(8,128)(2,1)} %tokens.1, bf16[8192,256]{1,0:T(8,128)(2,1)} %w_latent.1, bf16[8,256,256]{2,1,0:T(8,128)(2,1)} %bitcast.4, ...), custom_call_target="tpu_custom_call" | custom-call | flops 3758096384 | bytes 10485760 | tf_op jit(solution)/shard_map/pallas_call | solution.py:560
  103.8 2.3 %shard_map.120 = (bf16[32,256]{1,0:T(8,128)(2,1)}, bf16[32,256]{1,0:T(8,128)(2,1)}, bf16[1,1024,256]{2,1,0:T(8,128)(2,1)}, bf16[1,1024,256]{2,1,0:T(8,128)(2,1)}, bf16[1,256,1024]{2,1,0:T(8,128)(2,1)}) custom-call(bf16[32,256]{1,0:T(8,128)(2,1)} %get-tuple-element.10.refs_0_, bf16[32,256]{1,0:T(8,128)(2,1)} %get-tuple-element.11.refs_1_, ...), custom_call_target="tpu_custom_call" | custom-call | tf_op jit(solution)/shard_map/pallas_call | solution.py:635
